TPU v7x, 256 devices: a whole 4x4x8 slice. The times are simulated.
256 devices in a mesh: dp: 32 (over y, x, core), mp: 8 (over z).
Axes of the slice: x: 4, y: 4, z: 8, core: 2. Of those that a mesh axis runs over, the one named last changes fastest.
Arguments:
- grads: bfloat16 [32, 1024, 1024], P('dp', None, 'mp')
- momentum: float32 [32, 1024, 1024], P('dp', None, 'mp'), may hold values from -6 to 6
- second_moment: float32 [32, 1024, 1024], P('dp', None, 'mp'), may hold values from 0.0001 to 0.01
- owners: int32 [32], replicated, may hold values from 0 to 31, as said below
- left_stats: float32 [32, 3, 1024, 1024], P('dp', None, 'mp'), may hold values from -6 to 6
- right_stats: float32 [32, 3, 1024, 1024], P('dp', None, 'mp'), may hold values from -6 to 6
- left_roots: bfloat16 [32, 3, 1024, 1024], P('dp', None, None, 'mp'), as said below
- right_roots: bfloat16 [32, 3, 1024, 1024], P('dp', None, None, 'mp'), as said below
Outputs:
- step: bfloat16 [32, 1024, 1024], P('dp', None, 'mp')
- momentum_out: float32 [32, 1024, 1024], P('dp', None, 'mp')
- left_out: float32 [32, 3, 1024, 1024], P('dp', None, 'mp')
- right_out: float32 [32, 3, 1024, 1024], P('dp', None, 'mp')
Inputs may be any that keep to these rules, and one draw needn't show every extreme that they name: `owners`: each owner index appears at most 3 times, and one appears exactly 3 times. `left_roots`: each 1024 x 1024 block is symmetric. `right_roots`: each 1024 x 1024 block is symmetric.
All inputs are finite; a program needn't handle non-finite values.
Results may differ from a plain program's by a relative error of at most 0.0022.
Values may be sent and summed in bfloat16 or wider, within the bound.
A program may use at most 128 MiB of HBM per device.

v0:
```python
import jax
import jax.numpy as jnp
from jax import lax
from jax.sharding import PartitionSpec as P

beta_one = 0.9
beta_adam = 0.99
beta_stat = 0.95
adam_eps = 1e-08
norm_eps = 1e-06
step_rate = 0.5


def slot_table(owners):
    positions = jnp.arange(owners.shape[0], dtype=jnp.int32)
    same_owner = owners[:, None] == owners[None, :]
    earlier = positions[None, :] < positions[:, None]
    return jnp.sum((same_owner & earlier).astype(jnp.int32), axis=1)


def body(grads, momentum, second_moment, owners, left_stats, right_stats, left_roots, right_roots):
    own_index = lax.axis_index("dp")
    per_device = grads.shape[0]
    block_size = grads.shape[1]
    col_part = grads.shape[2]
    slot_count = left_stats.shape[1]
    block_count = owners.shape[0]
    slot_of = slot_table(owners)
    block_ids = jnp.arange(block_count, dtype=jnp.int32)
    holder_of = block_ids // per_device
    same_pair = (owners[:, None] == owners[None, :]) & (holder_of[:, None] == holder_of[None, :])
    same_pair = same_pair & (block_ids[None, :] < block_ids[:, None])
    grad_wide = grads.astype(jnp.float32)
    second_new = beta_adam * second_moment + (1.0 - beta_adam) * grad_wide * grad_wide
    adam_dir = grad_wide / (jnp.sqrt(second_new) + adam_eps)
    adam_sq = lax.psum(jnp.sum(adam_dir * adam_dir, axis=(1, 2)), "mp").astype(jnp.bfloat16)
    slot_ids = jnp.arange(slot_count, dtype=jnp.int32)
    owned_slot = (owners[None, :] == own_index) & (slot_of[None, :] == slot_ids[:, None])
    filled = jnp.any(owned_slot, axis=1)
    slot_block = jnp.sum(jnp.where(owned_slot, block_ids[None, :], 0), axis=1)
    initial = (
        jnp.zeros((slot_count, block_size, col_part), jnp.bfloat16),
        jnp.zeros((slot_count,), jnp.bfloat16),
    )
    pieces = (
        lax.all_gather(grads, "dp", axis=0, tiled=True),
        lax.all_gather(adam_sq, "dp", axis=0, tiled=True),
    )
    piece_count = pieces[0].shape[0]
    inside = filled & (slot_block >= 0) & (slot_block < piece_count)
    local_index = jnp.clip(slot_block, 0, piece_count - 1)
    kept_grad = jnp.where(inside[:, None, None], pieces[0][local_index], initial[0])
    kept_norm = jnp.where(inside, pieces[1][local_index], initial[1])
    row_start = lax.axis_index("mp") * col_part
    right_local = right_roots[0]
    left_local = left_roots[0]
    piece = lax.all_gather(kept_grad, "mp", axis=2, tiled=True)
    own_rows = lax.dynamic_slice_in_dim(piece, row_start, col_part, 1)
    left_acc = jnp.einsum("src,swc->srw", own_rows, piece, preferred_element_type=jnp.float32)
    right_part = jnp.einsum("swr,swc->src", kept_grad, piece, preferred_element_type=jnp.float32)
    mixed_acc = jnp.einsum("swc,scr->swr", piece, right_local, preferred_element_type=jnp.float32)
    mixed = mixed_acc.astype(jnp.bfloat16)
    piece = lax.all_gather(left_local, "mp", axis=2, tiled=True)
    precond = jnp.einsum("swc,scr->swr", piece, mixed, preferred_element_type=jnp.float32)
    precond_sq = lax.psum(jnp.sum(precond * precond, axis=(1, 2)), "mp")
    graft_scale = jnp.sqrt(kept_norm.astype(jnp.float32) / (precond_sq + norm_eps))
    graft_dir = (precond * graft_scale[:, None, None]).astype(jnp.bfloat16)
    return_hot = (block_ids[:, None] == slot_block[None, :]) & filled[None, :]
    owner_term = jnp.einsum(
        "bs,swr->bwr",
        return_hot.astype(jnp.bfloat16),
        graft_dir,
        preferred_element_type=jnp.float32,
    )
    returned = lax.psum_scatter(
        owner_term.astype(jnp.bfloat16), "dp", scatter_dimension=0, tiled=True
    ).astype(jnp.float32)
    momentum_out = beta_one * momentum + (1.0 - beta_one) * returned
    step = (-step_rate * momentum_out).astype(jnp.bfloat16)
    left_out = beta_stat * left_stats + (1.0 - beta_stat) * left_acc[None]
    right_out = beta_stat * right_stats + (1.0 - beta_stat) * right_part[None]
    return (step, momentum_out, left_out, right_out)


def solution(mesh):
    return jax.shard_map(
        body,
        mesh=mesh,
        in_specs=(
            P("dp", None, "mp"),
            P("dp", None, "mp"),
            P("dp", None, "mp"),
            P(),
            P("dp", None, "mp", None),
            P("dp", None, "mp", None),
            P("dp", None, None, "mp"),
            P("dp", None, None, "mp"),
        ),
        out_specs=(
            P("dp", None, "mp"),
            P("dp", None, "mp"),
            P("dp", None, "mp", None),
            P("dp", None, "mp", None),
        ),
        check_vma=False,
    )
```

profile of v0, /device:TPU:1, one launch (start us, length us, event | category | flops | bytes accessed | tf_op | source)
XLA Modules:
  0.0 445.9 jit_solution(4819947525284424260)
XLA Ops:
  7.2 0.7 all-gather.5.cloned.1.call-update
  8.0 0.7 all-gather.9.cloned.1.call-update
  8.7 0.9 convert_reduce_fusion
  9.6 0.7 broadcast_compare_fusion
  10.6 62.2 %all-gather.5.cloned.1.call-done = bf16[32,1024,128]{2,1,0:T(8,128)(2,1)} async-done(((bf16[1,1024,128]{2,1,0:T(8,128)(2,1)}), bf16[32,1024,128]{2,1,0:T(8,128)(2,1)}) %all-gather.5.cloned.1.call-update) | async-done | bytes 8388624 | tf_op jit(solution)/shard_map/all_gather | solution.py:46
  72.7 4.1 gather_fusion
  76.9 1.0 broadcast_select_fusion
  78.0 0.6 dynamic-slice
  78.5 0.9 fusion.11
  79.4 72.3 %all-gather.9.cloned.1.call-done = bf16[1,3,1024,1024]{3,2,1,0:T(8,128)(2,1)} async-done(((bf16[1,3,1024,128]{3,2,1,0:T(8,128)(2,1)}), bf16[1,3,1024,1024]{3,2,1,0:T(8,128)(2,1)}) %all-gather.9.cloned.1.call-update) | async-done | bytes 6291472 | tf_op jit(solution)/shard_map/all_gather | solution.py:63
  151.7 81.4 %all-gather.7.cloned.1.call-done = bf16[3,1024,1024]{2,1,0:T(8,128)(2,1)} async-done(((bf16[3,1024,128]{2,1,0:T(8,128)(2,1)}), bf16[3,1024,1024]{2,1,0:T(8,128)(2,1)}) %all-gather.7.cloned.1.call-update) | async-done | bytes 6291472 | tf_op jit(solution)/shard_map/all_gather | solution.py:57
  233.1 9.4 %multiply_reduce_fusion = (f32[3]{0:T(128)S(1)}, f32[3,128,1024]{2,1,0:T(8,128)}) fusion(bf16[1,3,1024,1024]{3,2,1,0:T(8,128)(2,1)} %all-gather.9.cloned.1.call-done, bf16[3,1024,1024]{2,1,0:T(8,128)(2,1)} %all-gather.7.cloned.1.call-done, bf16[1,3,1024,128]{3,2,1,0:T(8,128)(2,1)S(1)} %copy-done), kind=kOutput, calls=%fused_computation.8 | convolution fusion | flops 1611792384 | bytes 14942220 | tf_op jit(solution)/shard_map/swc,scr->swr/dot_general | solution.py:64
  242.5 13.2 %all-reduce.1 = (f32[3]{0:T(128)S(1)}, bf16[1]{0:T(256)(128)(2,1)}) all-reduce(f32[3]{0:T(128)S(1)} %get-tuple-element.16, f32[1]{0:T(128)} %bitcast.5), channel_id=1, replica_groups=mesh['dp'=32,'mp'=8] {'mp'}, use_global_device_ids=true, to_apply=%region_6.7 | all-reduce | flops 4 | bytes 30 | tf_op jit(solution)/shard_map/psum | solution.py:65
  255.7 1.4 dynamic-update-slice
  257.1 70.0 %all-reduce = bf16[32]{0:T(256)(128)(2,1)S(1)} all-reduce(bf16[32]{0:T(256)(128)(2,1)S(1)} %dynamic-update-slice), channel_id=1, replica_groups=mesh['dp'=32,'mp'=8] {'dp'}, use_global_device_ids=true, to_apply=%add | all-reduce | flops 32 | bytes 128
  327.1 0.6 gather_fusion.1
  327.7 1.6 fusion.2
  329.4 0.7 copy.29
  330.1 4.7 %convolution_convert_fusion = bf16[32,1024,128]{2,0,1:T(8,128)(2,1)} fusion(bf16[3,1024,128]{2,0,1:T(4,128)(2,1)S(1)} %copy.29, s32[3]{0:T(128)S(1)} %select_reduce_fusion, pred[3]{0:T(512)(128)(4,1)S(1)} %fusion.17), kind=kOutput, calls=%fused_computation.2 | convolution fusion | flops 29360320 | bytes 9175055 | tf_op jit(solution)/shard_map/bs,swr->bwr/dot_general | solution.py:69
  334.9 9.8 %copy.30 = bf16[32,1024,128]{2,1,0:T(8,128)(2,1)} copy(bf16[32,1024,128]{2,0,1:T(8,128)(2,1)} %convolution_convert_fusion) | data formatting | bytes 16777216 | tf_op jit(solution)/shard_map/convert_element_type | solution.py:76
  344.8 7.0 %bitcast_add_fusion.1 = f32[1,3,128,1024]{3,2,1,0:T(8,128)} fusion(f32[1,3,128,1024]{3,2,1,0:T(8,128)} %param.12, bf16[3,1024,1024]{2,1,0:T(8,128)(2,1)} %all-gather.7.cloned.1.call-done, s32[]{:T(128)S(6)} %select_n.30), kind=kOutput, calls=%fused_computation.6 | convolution fusion | flops 806486016 | bytes 10223620 | tf_op jit(solution)/shard_map/src,swc->srw/dot_general | solution.py:59
  351.8 2.5 bitcast_add_fusion
  354.3 83.2 %reduce-scatter.2.cloned.1.call-done = bf16[1,1024,128]{2,1,0:T(8,128)(2,1)} async-done(((bf16[32,1024,128]{2,1,0:T(8,128)(2,1)}), bf16[1,1024,128]{2,1,0:T(8,128)(2,1)}) %reduce-scatter.2.cloned.1.call-update) | async-done | bytes 262160 | tf_op jit(solution)/shard_map/reduce_scatter | solution.py:75
  437.5 1.9 multiply_convert_fusion.1
  (32 shorter events, 0.5 us)
Async XLA Ops:
  7.2 226.0 %copy-start = (bf16[1,3,1024,128]{3,2,1,0:T(8,128)(2,1)S(1)}, bf16[1,3,1024,128]{3,2,1,0:T(8,128)(2,1)}, u32[]{:S(2)}) copy-start(bf16[1,3,1024,128]{3,2,1,0:T(8,128)(2,1)} %param.15) | copy-start | bytes 2359300
  7.2 65.6 %all-gather.5.cloned.1.call-start = ((), (), s32[]{:S(2)}) async-start(), calls=%async_computation.1 | async-start | bytes 8650752 | tf_op jit(solution)/shard_map/all_gather | solution.py:46
  7.9 143.8 %all-gather.9.cloned.1.call-start = ((), (), s32[]{:S(2)}) async-start(), calls=%async_computation.4 | async-start | bytes 7077888 | tf_op jit(solution)/shard_map/all_gather | solution.py:63
  8.7 224.5 %all-gather.7.cloned.1.call-start = ((), (), s32[]{:S(2)}) async-start(), calls=%async_computation.2 | async-start | bytes 7077888 | tf_op jit(solution)/shard_map/all_gather | solution.py:57
  76.8 1.1 copy-start.6
  76.8 1.7 copy-start.3
  76.8 1.7 copy-start.5
  77.9 359.6 %reduce-scatter.2.cloned.1.call-start = ((), (), s32[]{:S(2)}) async-start(), calls=%async_computation.3 | async-start | bytes 8650752 | tf_op jit(solution)/shard_map/reduce_scatter | solution.py:75
  344.7 7.1 %slice-start = ((s8[6291456]{0:T(1024)(128)(4,1)}), s8[2097152]{0:T(1024)(128)(4,1)S(1)}, s32[]{:S(2)}) async-start(s8[6291456]{0:T(1024)(128)(4,1)} %bitcast.32), calls=%async_computation.5 | async-start | bytes 4194304
  344.7 7.0 %slice-start.1 = ((s8[6291456]{0:T(1024)(128)(4,1)}), s8[4194304]{0:T(1024)(128)(4,1)S(1)}, s32[]{:S(2)}) async-start(s8[6291456]{0:T(1024)(128)(4,1)} %bitcast.32), calls=%async_computation.6 | async-start | bytes 8388608
  344.8 7.0 %copy-start.1 = (bf16[3,1024,128]{2,1,0:T(8,128)(2,1)S(1)}, bf16[3,1024,128]{2,1,0:T(8,128)(2,1)}, u32[]{:S(2)}) copy-start(bf16[3,1024,128]{2,1,0:T(8,128)(2,1)} %broadcast_select_fusion) | copy-start | bytes 2359300
  344.8 7.0 %copy-start.2 = (f32[1,3,128,1024]{3,2,1,0:T(8,128)S(1)}, f32[1,3,128,1024]{3,2,1,0:T(8,128)}, u32[]{:S(2)}) copy-start(f32[1,3,128,1024]{3,2,1,0:T(8,128)} %param.13) | copy-start | bytes 4718596
  351.8 85.7 %copy-start.4 = (f32[1,1024,128]{2,1,0:T(8,128)S(1)}, f32[1,1024,128]{2,1,0:T(8,128)}, u32[]{:S(2)}) copy-start(f32[1,1024,128]{2,1,0:T(8,128)} %param.9) | copy-start | bytes 1572868
Sparse Core Ops, SparseCore 0:
  10.6 62.1 all-gather.4
  74.4 77.2 all-gather.8
  153.4 79.6 all-gather.6
  344.9 92.5 reduce-scatter.1
where the time goes:
time: 447 us; the launch traced here: 446 us
  waiting for transfers between devices  300 us (67%)
  blocking collectives  83.1 us (19%)
  matrix products  23.6 us (5%)
  local copies, waits for them, and re-layouts  17.3 us (4%)
  between operations  13.9 us (3%)
  other arithmetic  7.32 us (2%)
    reduce_scatter x1, waiting for transfers between devices, body(): lax.psum_scatter(owner_term.astype(jnp.bfloat16), 'dp', scatter_dimension...  83.2 us
    all_gather x1, waiting for transfers between devices, body(): piece = lax.all_gather(kept_grad, 'mp', axis=2, tiled=True)  81.4 us
    all_gather x1, waiting for transfers between devices, body(): piece = lax.all_gather(left_local, 'mp', axis=2, tiled=True)  72.3 us
    unnamed x1, blocking collectives  70 us
    all_gather x1, waiting for transfers between devices, body(): lax.all_gather(grads, 'dp', axis=0, tiled=True)  62.2 us
    psum x1, blocking collectives, body(): precond_sq = lax.psum(jnp.sum(precond * precond, axis=(1, 2)), 'mp')  13.2 us
    convert_element_type x1, local copies, waits for them, and re-layouts, body(): owner_term.astype(jnp.bfloat16)  9.84 us
    dot_general x1, matrix products, body(): jnp.einsum('swc,scr->swr', piece, mixed, preferred_element_type=jnp.float32)  9.41 us
  transfers between devices with their start and end apart: 4, of which 4 were waited for; matrix products, arithmetic and copies ran while one was open for 4% of the time, Pallas kernels for 0%

commit v1 on v0

v1 whole, which is shorter than its diff:
```python
import jax
import jax.numpy as jnp
from jax import lax
from jax.experimental import pallas as pl
from jax.experimental.pallas import tpu as pltpu
from jax.sharding import PartitionSpec as P

beta_one = 0.9
beta_adam = 0.99
beta_stat = 0.95
adam_eps = 1e-08
norm_eps = 1e-06
step_rate = 0.5

MESH = pl.DeviceIdType.MESH
NZ = 8
NG = 8
NT = 4
NS = 3
TILE = 128
BS = 1024
HALF = 5 * TILE
PIECE = HALF // NG
CH = 4
F32 = jnp.float32
BF16 = jnp.bfloat16


def dot(a, b, ca=1, cb=0):
    return lax.dot_general(a, b, (((ca,), (cb,)), ((), ())), preferred_element_type=F32)


def kernel(
    tbl, grads, second, left_roots, right_roots,
    graft, gram_l, gram_r,
    gbuf, sec, l_rot,
    a_r, a_l, t_r, t_l, b_r, b_l, c_r, c_l, d_r, d_l,
    l_all, rg, lg, f_r, f_l, h_r, h_l, acc, mext, gt, pre, ps,
    local_sem, zg_s, zg_r, zl_s, zl_r, ps_s, ps_r, s1_s, s1_r, s2_s, s2_r, s3_s, s3_r, g1_s, g1_r, g2_s, g2_r, g3_s, g3_r,
):
    d = lax.axis_index("dp")
    z = lax.axis_index("mp")
    core = d % 2
    x = (d // 2) % 4
    y = d // 8

    g_of = (x * 2 + core, y * 2 + core)
    t_of = (y, x)

    def dev(mode, g, t):
        if mode == 0:
            return t * 8 + g
        return (g // 2) * 8 + t * 2 + g % 2

    def group(mode, k):
        g = (g_of[mode] + k) % NG
        return g, dev(mode, g, t_of[mode])

    def other(mode, k):
        t = (t_of[mode] + k) % NT
        return t, dev(mode, g_of[mode], t)

    def remote(src, dst, ss, rs, to, zto):
        return pltpu.make_async_remote_copy(
            src_ref=src, dst_ref=dst, send_sem=ss, recv_sem=rs, device_id=(to, zto), device_id_type=MESH
        )

    sent = []

    def start(copy):
        copy.start()
        sent.append(copy)
        return copy

    own_g = pltpu.make_async_copy(grads.at[0], gbuf.at[z], local_sem.at[0])
    own_g.start()
    rot = []
    for j in range(5):
        row = pl.multiple_of(((z + j) % NZ) * TILE, TILE)
        copy = pltpu.make_async_copy(
            left_roots.at[0, :, pl.ds(row, TILE), :], l_rot.at[:, pl.ds(j * TILE, TILE), :], local_sem.at[1 + j]
        )
        copy.start()
        rot.append(copy)
    own_r = pltpu.make_async_copy(
        right_roots.at[0, :, pl.ds(pl.multiple_of(g_of[0] * TILE, TILE), TILE), :],
        a_r.at[pl.ds(g_of[0] * NS, NS)],
        local_sem.at[6],
    )
    own_r.start()
    own_sec = pltpu.make_async_copy(second.at[0], sec, local_sem.at[7])
    own_sec.start()

    barrier = pltpu.get_barrier_semaphore()
    partners = [(d, (z + k) % NZ) for k in range(1, NZ)]
    partners += [(group(0, k)[1], z) for k in range(1, NG)]
    for k in range(1, NT):
        for cc in range(2):
            partners.append((((y + k) % 4) * 8 + x * 2 + cc, z))
    for p in partners:
        pl.semaphore_signal(barrier, inc=1, device_id=p, device_id_type=MESH)
    pl.semaphore_wait(barrier, len(partners))

    right, left = (z + 1) % NZ, (z + NZ - 1) % NZ

    def ring(buf, rows, ss, rs, first):
        part = rows // CH

        def copy(direction, s, c):
            slot = (z + NZ - s) % NZ if direction == 0 else (z + s) % NZ
            i = (direction * 4 + s) * CH + c
            span = pl.ds(c * part, part)
            src = first(span) if s == 0 else buf.at[slot, span, :]
            to = right if direction == 0 else left
            return remote(src, buf.at[slot, span, :], ss.at[i], rs.at[i], d, to)

        def last_dir(c):
            return 0 if c < CH // 2 else 1

        def begin():
            for c in range(CH):
                start(copy(0, 0, c))
                start(copy(1, 0, c))

        def relay(s):
            for c in range(CH):
                for direction in range(2):
                    copy(direction, s - 1, c).wait_recv()
                    if s < 3 or last_dir(c) == direction:
                        start(copy(direction, s, c))

        def finish():
            for c in range(CH):
                copy(last_dir(c), 3, c).wait_recv()

        return begin, relay, finish

    zg_begin, zg_relay, zg_finish = ring(gbuf, BS, zg_s, zg_r, lambda span: grads.at[0, span, :])
    zg_begin()

    for copy in rot:
        copy.wait()
    own_l = pltpu.make_async_copy(
        l_rot.at[:, pl.ds(pl.multiple_of(g_of[1] * PIECE, 16), PIECE), :],
        a_l.at[pl.ds(g_of[1] * NS, NS)],
        local_sem.at[8],
    )
    own_l.start()

    def s1(mode, k):
        g, to = group(mode, k)
        i = mode * NG + k
        if mode == 0:
            src = right_roots.at[0, :, pl.ds(pl.multiple_of(g * TILE, TILE), TILE), :]
        else:
            src = l_rot.at[:, pl.ds(pl.multiple_of(g * PIECE, 16), PIECE), :]
        dst = (a_r, a_l)[mode].at[pl.ds(g_of[mode] * NS, NS)]
        return remote(src, dst, s1_s.at[i], s1_r.at[i], to, z)

    for k in range(1, NG):
        start(s1(1, k))
        start(s1(0, k))

    own_g.wait()
    own_sec.wait()

    def adam_rows(i, total):
        rows = pl.ds(pl.multiple_of(i * TILE, TILE), TILE)
        g = gbuf[z, rows, :].astype(F32)
        new = beta_adam * sec[rows, :] + (1.0 - beta_adam) * g * g
        direction = g / (jnp.sqrt(new) + adam_eps)
        return total + jnp.sum((direction * direction).reshape(TILE // 8, 8, TILE), axis=0)

    adam_part = lax.fori_loop(0, BS // TILE, adam_rows, jnp.zeros((8, TILE), F32))

    def share(which, part):
        ps[which, z] = part
        copies = []
        for k in range(1, NZ):
            i = which * NZ + k
            copies.append(start(remote(ps.at[which, z], ps.at[which, z], ps_s.at[i], ps_r.at[i], d, (z + k) % NZ)))
        return copies

    adam_copies = share(0, adam_part)
    gt[...] = gbuf[z].T

    zg_relay(1)

    def s2(mode, k):
        t, to = other(mode, k)
        i = mode * NT + k
        dst = (b_r, b_l)[mode].at[pl.ds(t_of[mode] * NG, NG)]
        return remote((t_r, t_l)[mode].at[pl.ds((k - 1) * NG, NG)], dst, s2_s.at[i], s2_r.at[i], to, z)

    def s1_to_s2(mode):
        (own_r, own_l)[mode].wait()
        for k in range(1, NG):
            s1(mode, k).wait_recv()
        a, t_buf, b = ((a_r, t_r, b_r), (a_l, t_l, b_l))[mode]
        for k in (1, 3, 2, 0):
            t, _ = other(mode, k)

            def choose(g, _):
                index = tbl[mode, 0, dev(mode, g, t)]
                if k == 0:
                    b[t * NG + g] = a[index]
                else:
                    t_buf[(k - 1) * NG + g] = a[index]
                return 0

            lax.fori_loop(0, NG, choose, 0)
            if k:
                start(s2(mode, k))

    s1_to_s2(1)
    s1_to_s2(0)
    zg_relay(2)
    zg_relay(3)

    def s3(mode, k):
        g, to = group(mode, k)
        i = mode * NG + k
        dst = (d_r.at[g_of[mode]], d_l.at[pl.ds(pl.multiple_of(g_of[mode] * PIECE, 16), PIECE), :])[mode]
        return remote((c_r, c_l)[mode].at[k], dst, s3_s.at[i], s3_r.at[i], to, z)

    def s2_to_s3(mode):
        for k in range(1, NT):
            s2(mode, k).wait_recv()
        b, c_buf = ((b_r, c_r), (b_l, c_l))[mode]
        for k in range(NG):
            g, to = group(mode, k)
            value = b[tbl[mode, 1, to] * NG + g]
            if k:
                c_buf[k] = value
                start(s3(mode, k))
            elif mode == 0:
                d_r[g] = value
            else:
                d_l[pl.ds(pl.multiple_of(g * PIECE, 16), PIECE), :] = value

    def s3_done(mode):
        for k in range(1, NG):
            s3(mode, k).wait_recv()

    s2_to_s3(1)
    s2_to_s3(0)
    zg_finish()

    def g1(mode, k):
        g, to = group(mode, k)
        i = mode * NG + k
        dst = (f_r, f_l)[mode].at[t_of[mode] * NG + g_of[mode]]
        return remote((rg, lg)[mode].at[g], dst, g1_s.at[i], g1_r.at[i], to, z)

    def left_tile(i, _):
        total = jnp.zeros((TILE, TILE), F32)
        for c in range(NZ):
            own_rows = gbuf[c, pl.ds(pl.multiple_of(z * TILE, TILE), TILE), :]
            rows = gbuf[c, pl.ds(pl.multiple_of(i * TILE, TILE), TILE), :]
            total = total + dot(own_rows, rows, 1, 1)
        lg[i] = total.astype(BF16)
        return 0

    def right_tile(i, _):
        rg[i] = dot(gt[...], gbuf[i]).astype(BF16)
        return 0

    lax.fori_loop(0, NG, left_tile, 0)
    for k in range(1, NG):
        start(g1(1, k))
    f_l[t_of[1] * NG + g_of[1]] = lg[g_of[1]]
    lax.fori_loop(0, NG, right_tile, 0)
    for k in range(1, NG):
        start(g1(0, k))
    f_r[t_of[0] * NG + g_of[0]] = rg[g_of[0]]

    s3_done(1)
    zl_begin, zl_relay, zl_finish = ring(l_all, HALF, zl_s, zl_r, lambda span: d_l.at[span, :])
    zl_begin()

    s3_done(0)
    acc[...] = dot(gbuf[0], d_r[0])

    def mix(c, _):
        acc[...] += dot(gbuf[c], d_r[c])
        return 0

    lax.fori_loop(1, NZ, mix, 0)
    for j in range(11):
        mext[j] = acc[(j % NZ) * TILE:(j % NZ + 1) * TILE, :].astype(BF16)

    def g2(mode, k):
        t, to = other(mode, k)
        i = mode * NT + k
        mine = (f_r, f_l)[mode].at[pl.ds(t_of[mode] * NG, NG)]
        return remote(mine, mine, g2_s.at[i], g2_r.at[i], to, z)

    def g1_to_g2(mode):
        for k in range(1, NG):
            g1(mode, k).wait_recv()
        for k in (1, 3, 2):
            start(g2(mode, k))

    g1_to_g2(1)
    g1_to_g2(0)

    pre[...] = jnp.zeros((NZ, TILE, TILE), F32)

    def add_shard(shard, s):
        direct = dot(shard, mext[s])
        for j in range(5):
            row = (s + j) % NZ
            pre[row] += direct[j * TILE:(j + 1) * TILE, :]
        three = mext[pl.ds(s + 1, 3)].reshape(3 * TILE, TILE)
        pre[s] += dot(shard[TILE:4 * TILE, :], three, 0, 0)

    add_shard(d_l[...], z)
    zl_relay(1)
    add_shard(l_all[left], left)
    add_shard(l_all[right], right)
    zl_relay(2)

    def g3(mode, k):
        g, to = group(mode, k)
        i = mode * NG + k
        dst = (gram_r, gram_l)[mode].at[g_of[mode]]
        return remote((h_r, h_l)[mode].at[k], dst, g3_s.at[i], g3_r.at[i], to, z)

    def g2_to_g3(mode):
        for k in range(1, NT):
            g2(mode, k).wait_recv()
        f, h, out = ((f_r, h_r, gram_r), (f_l, h_l, gram_l))[mode]
        for k in range(NG):
            g, to = group(mode, k)
            for q in range(NS):
                value = f[tbl[mode, 2 + q, to]]
                if k:
                    h[k, q] = value
                else:
                    out[g, q] = value
            if k:
                start(g3(mode, k))

    add_shard(l_all[(z + 6) % NZ], (z + 6) % NZ)
    add_shard(l_all[(z + 2) % NZ], (z + 2) % NZ)
    zl_relay(3)
    g2_to_g3(1)
    g2_to_g3(0)
    add_shard(l_all[(z + 5) % NZ], (z + 5) % NZ)
    add_shard(l_all[(z + 3) % NZ], (z + 3) % NZ)
    zl_finish()
    add_shard(l_all[(z + 4) % NZ], (z + 4) % NZ)

    squares = jnp.zeros((8, TILE), F32)
    for a in range(NZ):
        rows = pre[a]
        squares = squares + jnp.sum((rows * rows).reshape(TILE // 8, 8, TILE), axis=0)
    norm_copies = share(1, squares)
    for copy in adam_copies + norm_copies:
        copy.wait_recv()

    def total(which):
        rows = jnp.sum(ps[which], axis=0)
        return jnp.sum(jnp.sum(rows, axis=0, keepdims=True), axis=1, keepdims=True)

    adam_sq = total(0).astype(BF16).astype(F32)
    scale = jnp.sqrt(adam_sq / (total(1) + norm_eps))
    for a in range(NZ):
        graft[a * TILE:(a + 1) * TILE, :] = (pre[a] * scale).astype(BF16)

    for mode in (1, 0):
        for k in range(1, NG):
            g3(mode, k).wait_recv()
    for copy in sent:
        copy.wait_send()


def update(filled, graft, momentum, gram_l, gram_r, left_stats, right_stats, step, momentum_out, left_out, right_out):
    new = beta_one * momentum[0] + (1.0 - beta_one) * graft[...].astype(F32)
    momentum_out[0] = new
    step[0] = (-step_rate * new).astype(BF16)
    for q in range(NS):
        on = filled[q] > 0
        for stats, gram, out in ((left_stats, gram_l, left_out), (right_stats, gram_r, right_out)):
            for c in range(NG):
                cols = slice(c * TILE, (c + 1) * TILE)
                term = jnp.where(on, gram[c, q].astype(F32), 0.0)
                out[0, q, :, cols] = beta_stat * stats[0, q, :, cols] + (1.0 - beta_stat) * term


def routes(owners):
    ids = jnp.arange(owners.shape[0], dtype=jnp.int32)
    same = owners[:, None] == owners[None, :]
    slot = jnp.sum((same & (ids[None, :] < ids[:, None])).astype(jnp.int32), axis=1)
    slots = jnp.arange(NS, dtype=jnp.int32)
    hit = (owners[None, None, :] == ids[None, :, None]) & (slot[None, None, :] == slots[:, None, None])
    block = jnp.sum(jnp.where(hit, ids[None, None, :], 0), axis=2)
    filled = jnp.any(hit, axis=2).astype(jnp.int32)

    def place(mode, i):
        if mode == 0:
            return i % 8, i // 8
        return (i // 8) * 2 + i % 2, (i // 2) % 4

    rows = []
    for mode in range(2):
        g, t = place(mode, owners)
        bg, bt = place(mode, block)
        rows.append(jnp.concatenate([(g * NS + slot)[None], t[None], bt * NG + bg], axis=0))
    return jnp.stack(rows), filled


def body(grads, momentum, second_moment, owners, left_stats, right_stats, left_roots, right_roots):
    tbl, filled = routes(owners)
    own = lax.dynamic_index_in_dim(filled, lax.axis_index("dp"), 1, keepdims=False)
    vmem = lambda shape, dtype=BF16: pltpu.VMEM(shape, dtype)
    dma = lambda n: pltpu.SemaphoreType.DMA((n,))
    any_spec = pl.BlockSpec(memory_space=pl.ANY)
    tile = (TILE, TILE)
    graft, gram_l, gram_r = pl.pallas_call(
        kernel,
        name="shampoo",
        out_shape=(
            jax.ShapeDtypeStruct((BS, TILE), BF16),
            jax.ShapeDtypeStruct((NG, NS) + tile, BF16),
            jax.ShapeDtypeStruct((NG, NS) + tile, BF16),
        ),
        in_specs=[pl.BlockSpec(memory_space=pltpu.SMEM)] + [any_spec] * 4,
        out_specs=[pl.BlockSpec(memory_space=pltpu.VMEM)] * 3,
        scratch_shapes=[
            vmem((NZ, BS, TILE)), vmem((BS, TILE), F32), vmem((NS, HALF, TILE)),
            vmem((NG * NS,) + tile), vmem((NG * NS, PIECE, TILE)),
            vmem((3 * NG,) + tile), vmem((3 * NG, PIECE, TILE)),
            vmem((NT * NG,) + tile), vmem((NT * NG, PIECE, TILE)),
            vmem((NG,) + tile), vmem((NG, PIECE, TILE)),
            vmem((NG,) + tile), vmem((HALF, TILE)),
            vmem((NZ, HALF, TILE)), vmem((NG,) + tile), vmem((NG,) + tile),
            vmem((NT * NG,) + tile), vmem((NT * NG,) + tile),
            vmem((NG, NS) + tile), vmem((NG, NS) + tile),
            vmem((BS, TILE), F32), vmem((11,) + tile), vmem((TILE, BS)), vmem((NZ,) + tile, F32), vmem((2, NZ, 8, TILE), F32),
            dma(9), dma(8 * CH), dma(8 * CH), dma(8 * CH), dma(8 * CH), dma(2 * NZ), dma(2 * NZ),
            dma(2 * NG), dma(2 * NG), dma(2 * NT), dma(2 * NT), dma(2 * NG), dma(2 * NG),
            dma(2 * NG), dma(2 * NG), dma(2 * NT), dma(2 * NT), dma(2 * NG), dma(2 * NG),
        ],
        compiler_params=pltpu.CompilerParams(collective_id=0, has_side_effects=True, vmem_limit_bytes=40 * 2**20),
    )(tbl, grads, second_moment, left_roots, right_roots)

    steps = 4
    rows, wide = TILE // steps, BS // steps
    slab = pl.BlockSpec((1, wide, TILE), lambda i: (0, i, 0))
    stats = pl.BlockSpec((1, NS, rows, BS), lambda i: (0, 0, i, 0))
    gram = pl.BlockSpec((NG, NS, rows, TILE), lambda i: (0, 0, i, 0))
    return pl.pallas_call(
        update,
        name="update",
        grid=(steps,),
        out_shape=(
            jax.ShapeDtypeStruct((1, BS, TILE), BF16),
            jax.ShapeDtypeStruct((1, BS, TILE), F32),
            jax.ShapeDtypeStruct((1, NS, TILE, BS), F32),
            jax.ShapeDtypeStruct((1, NS, TILE, BS), F32),
        ),
        in_specs=[
            pl.BlockSpec(memory_space=pltpu.SMEM),
            pl.BlockSpec((wide, TILE), lambda i: (i, 0)),
            slab, gram, gram, stats, stats,
        ],
        out_specs=(slab, slab, stats, stats),
        compiler_params=pltpu.CompilerParams(vmem_limit_bytes=40 * 2**20),
    )(own, graft, momentum, gram_l, gram_r, left_stats, right_stats)


def solution(mesh):
    return jax.shard_map(
        body,
        mesh=mesh,
        in_specs=(
            P("dp", None, "mp"),
            P("dp", None, "mp"),
            P("dp", None, "mp"),
            P(),
            P("dp", None, "mp", None),
            P("dp", None, "mp", None),
            P("dp", None, None, "mp"),
            P("dp", None, None, "mp"),
        ),
        out_specs=(
            P("dp", None, "mp"),
            P("dp", None, "mp"),
            P("dp", None, "mp", None),
            P("dp", None, "mp", None),
        ),
        check_vma=False,
    )
```

time: 447 us -> 86.4 us (0.19)
  waiting for transfers between devices: 300 us -> 0 us
  blocking collectives: 83.1 us -> 0 us
  Pallas kernels: 0 us -> 76.9 us
  matrix products: 23.6 us -> 0 us
  between operations: 13.9 us -> 0.71 us
  local copies, waits for them, and re-layouts: 17.3 us -> 5.85 us
  other arithmetic: 7.32 us -> 2.66 us
    all_gather x3 -> x0, waiting for transfers between devices: 216 us -> none  [the longest x1 81.4 us: body(): piece = lax.all_gather(kept_grad, 'mp', axis=2, tiled=True)]
    reduce_scatter x1 -> x0, waiting for transfers between devices: 83.2 us -> none  [body(): lax.psum_scatter(owner_term.astype(jnp.bfloat16), 'dp', scatter_dimension...]
    pallas_call x0 -> x2, Pallas kernels: none -> 76.9 us  [the longest x1 73.7 us: body(): pl.pallas_call(kernel, name='shampoo', out_shape=(jax.ShapeDtypeStruct((B...]
    unnamed x1 -> x0, blocking collectives: 70 us -> none
    dot_general x4 -> x0, matrix products: 23.6 us -> none  [the longest x1 9.41 us: body(): jnp.einsum('swc,scr->swr', piece, mixed, preferred_element_type=jnp.float32)]
    psum x1 -> x0, blocking collectives: 13.2 us -> none  [body(): precond_sq = lax.psum(jnp.sum(precond * precond, axis=(1, 2)), 'mp')]
    convert_element_type x2 -> x0, local copies, waits for them, and re-layouts: 10.6 us -> none  [the longest x1 9.84 us: body(): owner_term.astype(jnp.bfloat16)]
    gather x2 -> x0, local copies, waits for them, and re-layouts: 4.72 us -> none  [the longest x1 4.08 us: body(): pieces[0][local_index]]
  transfers between devices with their start and end apart: 4 -> 0, of which waited for: 4 -> 0; matrix products, arithmetic and copies ran while one was open for 4% -> 0% of each run, Pallas kernels for 0% -> 0%
where the time goes in v1:
time: 86.4 us; the launch traced here: 86.1 us
  Pallas kernels  76.9 us (89%)
  local copies, waits for them, and re-layouts  5.85 us (7%)
  other arithmetic  2.66 us (3%)
    pallas_call x1, Pallas kernels, body(): pl.pallas_call(kernel, name='shampoo', out_shape=(jax.ShapeDtypeStruct((B...  73.7 us
    unnamed x14, local copies, waits for them, and re-layouts  5.66 us
    pallas_call x1, Pallas kernels, body(): pl.pallas_call(update, name='update', grid=(steps,), out_shape=(jax.Shape...  3.14 us

profile of v1, /device:TPU:1, one launch (start us, length us, event | category | flops | bytes accessed | tf_op | source)
XLA Modules:
  0.0 86.1 jit_solution(4812703494416737922)
XLA Ops:
  0.6 0.0 copy-start
  0.6 1.0 %convert_reduce_fusion = s32[32]{0:T(128)S(1)} fusion(s32[32]{0:T(128)} %param.11), kind=kLoop, calls=%fused_computation.3 | loop fusion | flops 5088 | bytes 256 | tf_op jit(solution)/shard_map/reduce_sum | solution.py:394
  1.6 0.7 add_bitcast_fusion.2
  2.3 0.7 iota_compare_fusion.1
  3.0 0.2 and_reduce_fusion
  3.1 0.2 fusion
  3.3 0.2 dynamic-slice_reduce_fusion.filled
  3.5 0.0 copy-start.2
  3.5 1.1 %copy-done.2 = bf16[1,3,1024,128]{3,2,1,0:T(8,128)(2,1)S(1)} copy-done((bf16[1,3,1024,128]{3,2,1,0:T(8,128)(2,1)S(1)}, bf16[1,3,1024,128]{3,2,1,0:T(8,128)(2,1)}, u32[]{:S(2)}) %copy-start.2) | copy-done | bytes 786456
  4.7 0.0 copy-start.3
  4.7 1.1 %copy-done.3 = bf16[1,3,1024,128]{3,2,1,0:T(8,128)(2,1)S(1)} copy-done((bf16[1,3,1024,128]{3,2,1,0:T(8,128)(2,1)S(1)}, bf16[1,3,1024,128]{3,2,1,0:T(8,128)(2,1)}, u32[]{:S(2)}) %copy-start.3) | copy-done | bytes 786456
  5.8 0.0 copy-start.4
  5.8 1.0 %copy-done.4 = f32[1,1024,128]{2,1,0:T(8,128)S(1)} copy-done((f32[1,1024,128]{2,1,0:T(8,128)S(1)}, f32[1,1024,128]{2,1,0:T(8,128)}, u32[]{:S(2)}) %copy-start.4) | copy-done | bytes 524312
  6.8 0.0 copy-start.6
  6.8 0.9 %copy-done.6 = bf16[1,1024,128]{2,1,0:T(8,128)(2,1)S(1)} copy-done((bf16[1,1024,128]{2,1,0:T(8,128)(2,1)S(1)}, bf16[1,1024,128]{2,1,0:T(8,128)(2,1)}, u32[]{:S(2)}) %copy-start.6) | copy-done | bytes 262168
  7.8 0.0 copy-start.5
  7.8 73.7 %shampoo.1 = (bf16[1024,128]{1,0:T(8,128)(2,1)S(1)}, bf16[8,3,128,128]{3,2,1,0:T(8,128)(2,1)S(1)}, bf16[8,3,128,128]{3,2,1,0:T(8,128)(2,1)S(1)}) custom-call(s32[2,5,32]{2,1,0:T(8,128)S(1)} %pad_add_fusion.tbl, bf16[1,1024,128]{2,1,0:T(8,128)(2,1)S(1)} %copy-done.6, f32[1,1024,128]{2,1,0:T(8,128)S(1)} %copy-done.4, bf16[1,3,1024,128]{3,2,1,0:T(8,128)(2,1)S(1)} %copy-done.2, ...), custom_call_target="tpu_custom_call" | custom-call | tf_op jit(solution)/shard_map/shampoo/pallas_call | solution.py:420
  81.5 0.0 copy-done
  81.5 0.0 copy-done.5
  81.6 0.0 copy-start.1
  81.6 1.4 %copy-done.1 = f32[1,3,128,1024]{3,2,1,0:T(8,128)S(1)} copy-done((f32[1,3,128,1024]{3,2,1,0:T(8,128)S(1)}, f32[1,3,128,1024]{3,2,1,0:T(8,128)}, u32[]{:S(2)}) %copy-start.1) | copy-done | bytes 1572888
  83.0 3.1 %update.1 = (bf16[1,1024,128]{2,1,0:T(8,128)(2,1)}, f32[1,1024,128]{2,1,0:T(8,128)}, f32[1,3,128,1024]{3,2,1,0:T(8,128)}, f32[1,3,128,1024]{3,2,1,0:T(8,128)}) custom-call(s32[3]{0:T(128)S(1)} %dynamic-slice_reduce_fusion.filled, bf16[1024,128]{1,0:T(8,128)(2,1)S(1)} %get-tuple-element.7.graft, f32[1,1024,128]{2,1,0:T(8,128)S(1)} %copy-done.5, ...), custom_call_target="tpu_custom_call" | custom-call | tf_op jit(solution)/shard_map/update/pallas_call | solution.py:453
  (5 shorter events, 0.0 us)
Async XLA Ops:
  0.6 80.9 %copy-start = (f32[1,3,128,1024]{3,2,1,0:T(8,128)S(1)}, f32[1,3,128,1024]{3,2,1,0:T(8,128)}, u32[]{:S(2)}) copy-start(f32[1,3,128,1024]{3,2,1,0:T(8,128)} %left_stats.1) | copy-start | bytes 4718596
  3.5 1.1 %copy-start.2 = (bf16[1,3,1024,128]{3,2,1,0:T(8,128)(2,1)S(1)}, bf16[1,3,1024,128]{3,2,1,0:T(8,128)(2,1)}, u32[]{:S(2)}) copy-start(bf16[1,3,1024,128]{3,2,1,0:T(8,128)(2,1)} %left_roots.1) | copy-start | bytes 2359300
  4.7 1.1 %copy-start.3 = (bf16[1,3,1024,128]{3,2,1,0:T(8,128)(2,1)S(1)}, bf16[1,3,1024,128]{3,2,1,0:T(8,128)(2,1)}, u32[]{:S(2)}) copy-start(bf16[1,3,1024,128]{3,2,1,0:T(8,128)(2,1)} %right_roots.1) | copy-start | bytes 2359300
  5.8 1.0 %copy-start.4 = (f32[1,1024,128]{2,1,0:T(8,128)S(1)}, f32[1,1024,128]{2,1,0:T(8,128)}, u32[]{:S(2)}) copy-start(f32[1,1024,128]{2,1,0:T(8,128)} %second.1) | copy-start | bytes 1572868
  6.8 0.9 %copy-start.6 = (bf16[1,1024,128]{2,1,0:T(8,128)(2,1)S(1)}, bf16[1,1024,128]{2,1,0:T(8,128)(2,1)}, u32[]{:S(2)}) copy-start(bf16[1,1024,128]{2,1,0:T(8,128)(2,1)} %grads.1) | copy-start | bytes 786436
  7.8 73.8 %copy-start.5 = (f32[1,1024,128]{2,1,0:T(8,128)S(1)}, f32[1,1024,128]{2,1,0:T(8,128)}, u32[]{:S(2)}) copy-start(f32[1,1024,128]{2,1,0:T(8,128)} %momentum.1) | copy-start | bytes 1572868
  81.6 1.4 %copy-start.1 = (f32[1,3,128,1024]{3,2,1,0:T(8,128)S(1)}, f32[1,3,128,1024]{3,2,1,0:T(8,128)}, u32[]{:S(2)}) copy-start(f32[1,3,128,1024]{3,2,1,0:T(8,128)} %right_stats.1) | copy-start | bytes 4718596

commit v2 on v1

v2 whole, which is shorter than its diff:
```python
import jax
import jax.numpy as jnp
from jax import lax
from jax.experimental import pallas as pl
from jax.experimental.pallas import tpu as pltpu
from jax.sharding import PartitionSpec as P

beta_one = 0.9
beta_adam = 0.99
beta_stat = 0.95
adam_eps = 1e-08
norm_eps = 1e-06
step_rate = 0.5

MESH = pl.DeviceIdType.MESH
NZ = 8
NG = 8
NT = 4
NBLK = 32
NS = 3
TILE = 128
BS = 1024
HALF = 5 * TILE
PIECE = HALF // NG
CH = 2
F32 = jnp.float32
BF16 = jnp.bfloat16


def dot(a, b, ca=1, cb=0):
    return lax.dot_general(a, b, (((ca,), (cb,)), ((), ())), preferred_element_type=F32)


def place(mode, i):
    if mode == 0:
        return i & 7, i >> 3
    return (i >> 3) * 2 + (i & 1), (i >> 1) & 3


def kernel(
    owners, grads, second, left_roots, right_roots,
    graft, gram_l, gram_r,
    gbuf, sec, rot, a_r, a_l, t_buf, b_r, b_l, c_buf, strip, cross,
    l_all, gram, f_r, f_l, h, lacc, acc, mext, gt, pre, ps,
    slot_of, source, local_sem, xr_s, xr_r, zg_s, zg_r, zl_s, zl_r, ps_s, ps_r, s1_s, s1_r, s2_s, s2_r, s3_s, s3_r, g1_s, g1_r, g2_s, g2_r, g3_s, g3_r,
):
    a, b, f = (a_r, a_l), (b_r, b_l), (f_r, f_l)
    d = lax.axis_index("dp")
    z = lax.axis_index("mp")
    core = d % 2
    x = (d // 2) % 4
    y = d // 8

    g_of = (x * 2 + core, y * 2 + core)
    t_of = (y, x)

    def dev(mode, g, t):
        if mode == 0:
            return t * 8 + g
        return (g // 2) * 8 + t * 2 + g % 2

    def group(mode, k):
        g = (g_of[mode] + k) % NG
        return g, dev(mode, g, t_of[mode])

    def other(mode, k):
        t = (t_of[mode] + k) % NT
        return t, dev(mode, g_of[mode], t)

    def remote(src, dst, ss, rs, i, to, zto):
        return pltpu.make_async_remote_copy(
            src_ref=src, dst_ref=dst, send_sem=ss.at[i], recv_sem=rs.at[i], device_id=(to, zto), device_id_type=MESH
        )

    sent = []

    def start(copy):
        copy.start()
        sent.append(copy)
        return copy

    barrier = pltpu.get_barrier_semaphore()
    partners = [(d, (z + k) % NZ) for k in range(1, NZ)]
    partners += [(group(0, k)[1], z) for k in range(1, NG)]
    for k in range(1, NT):
        for cc in range(2):
            partners.append((((y + k) % 4) * 8 + x * 2 + cc, z))
    for p in partners:
        pl.semaphore_signal(barrier, inc=1, device_id=p, device_id_type=MESH)
    own_g = pltpu.make_async_copy(grads.at[0], gbuf.at[z], local_sem.at[0])
    own_g.start()
    strips = []
    for mode in (1, 0):
        for j in range(5):
            row = pl.multiple_of(((z + j) % NZ) * TILE, TILE)
            copy = pltpu.make_async_copy(
                (right_roots, left_roots)[mode].at[0, :, pl.ds(row, TILE), :],
                rot.at[mode, :, pl.ds(j * TILE, TILE), :],
                local_sem.at[4 + 5 * mode + j],
            )
            copy.start()
            strips.append(copy)
    own_sec = pltpu.make_async_copy(second.at[0], sec, local_sem.at[1])
    own_sec.start()

    pl.semaphore_wait(barrier, len(partners))

    right, left = (z + 1) % NZ, (z + NZ - 1) % NZ

    def ring(buf, rows, ss, rs, first):
        part = rows // CH

        def copy(direction, s, c):
            slot = (z + NZ - s) % NZ if direction == 0 else (z + s) % NZ
            i = (direction * 4 + s) * CH + c
            span = pl.ds(c * part, part)
            src = first(span) if s == 0 else buf.at[slot, span, :]
            to = right if direction == 0 else left
            return remote(src, buf.at[slot, span, :], ss, rs, i, d, to)

        def last_dir(c):
            return 0 if c < CH // 2 else 1

        def begin():
            for c in range(CH):
                start(copy(0, 0, c))
                start(copy(1, 0, c))

        def relay(s):
            for c in range(CH):
                for direction in range(2):
                    copy(direction, s - 1, c).wait_recv()
                    if s < 3 or last_dir(c) == direction:
                        start(copy(direction, s, c))

        def finish():
            for c in range(CH):
                copy(last_dir(c), 3, c).wait_recv()

        return begin, relay, finish

    zg_begin, zg_relay, zg_finish = ring(gbuf, BS, zg_s, zg_r, lambda span: grads.at[0, span, :])
    zg_begin()

    def find_slot(b, _):
        count = jnp.int32(0)
        for c in range(NBLK):
            count += jnp.where((owners[c] == owners[b]) & (c < b), 1, 0)
        slot_of[b] = jnp.minimum(count, NS - 1)
        return 0

    def find_blocks(i, _):
        for mode in range(2):
            o = dev(mode, i, t_of[mode])
            found = [jnp.int32(0)] * NS
            for b in range(NBLK):
                g, t = place(mode, b)
                mine = owners[b] == o
                for q in range(NS):
                    found[q] = jnp.where(mine & (slot_of[b] == q), t * NG + g, found[q])
            for q in range(NS):
                source[mode, i * NS + q] = found[q]
        return 0

    def piece(g):
        return pl.ds(pl.multiple_of(g * PIECE, 16), PIECE)

    def s1(mode, k):
        g, to = group(mode, k)
        dst = a[mode].at[pl.ds(g_of[mode] * NS, NS)]
        return remote(rot.at[mode, :, piece(g), :], dst, s1_s, s1_r, mode * NG + k, to, z)

    for copy in strips:
        copy.wait()
    own_pieces = []
    for mode in range(2):
        own_pieces.append(
            pltpu.make_async_copy(
                rot.at[mode, :, piece(g_of[mode]), :], a[mode].at[pl.ds(g_of[mode] * NS, NS)], local_sem.at[2 + mode]
            )
        )
        own_pieces[mode].start()
    for k in range(1, NG):
        start(s1(1, k))
        start(s1(0, k))

    own_g.wait()
    own_sec.wait()

    def adam_rows(i, total):
        rows = pl.ds(pl.multiple_of(i * TILE, TILE), TILE)
        g = gbuf[z, rows, :].astype(F32)
        new = beta_adam * sec[rows, :] + (1.0 - beta_adam) * g * g
        direction = g / (jnp.sqrt(new) + adam_eps)
        return total + jnp.sum((direction * direction).reshape(TILE // 8, 8, TILE), axis=0)

    adam_part = lax.fori_loop(0, BS // TILE, adam_rows, jnp.zeros((8, TILE), F32))

    def share(which, part):
        ps[which, z] = part
        copies = []
        for k in range(1, NZ):
            i = which * NZ + k
            copies.append(start(remote(ps.at[which, z], ps.at[which, z], ps_s, ps_r, i, d, (z + k) % NZ)))
        return copies

    adam_copies = share(0, adam_part)
    lax.fori_loop(0, NBLK, find_slot, 0)
    gt[...] = gbuf[z].T
    own_rows = pl.ds(pl.multiple_of(z * TILE, TILE), TILE)

    def add_gram(shard, first=False):
        gram[0, shard] = dot(gt[...], gbuf[shard]).astype(BF16)
        term = dot(gbuf[shard, own_rows, :], gbuf[shard], 1, 1)
        lacc[...] = term if first else lacc[...] + term

    add_gram(z, True)
    zg_relay(1)

    def s2(mode, k):
        t, to = other(mode, k)
        dst = b[mode].at[pl.ds(t_of[mode] * NG, NG)]
        return remote(t_buf.at[mode, pl.ds((k - 1) * NG, NG)], dst, s2_s, s2_r, mode * NT + k, to, z)

    def s1_to_s2(mode):
        own_pieces[mode].wait()
        for k in range(1, NG):
            s1(mode, k).wait_recv()
        for k in (1, 3, 2, 0):
            t, _ = other(mode, k)

            def choose(g, _):
                b_id = dev(mode, g, t)
                value = a[mode][place(mode, owners[b_id])[0] * NS + slot_of[b_id]]
                if k == 0:
                    b[mode][t * NG + g] = value
                else:
                    t_buf[mode, (k - 1) * NG + g] = value
                return 0

            lax.fori_loop(0, NG, choose, 0)
            if k:
                start(s2(mode, k))

    s1_to_s2(1)
    s1_to_s2(0)
    lax.fori_loop(0, NG, find_blocks, 0)
    add_gram(left)
    add_gram(right)
    zg_relay(2)
    add_gram((z + 6) % NZ)
    add_gram((z + 2) % NZ)
    zg_relay(3)
    add_gram((z + 5) % NZ)
    add_gram((z + 3) % NZ)

    def s3(mode, k):
        g, to = group(mode, k)
        return remote(
            c_buf.at[mode, k], strip.at[mode, piece(g_of[mode]), :], s3_s, s3_r, mode * NG + k, to, z
        )

    def s2_to_s3(mode):
        for k in range(1, NT):
            s2(mode, k).wait_recv()
        for k in range(NG):
            g, to = group(mode, k)
            value = b[mode][place(mode, owners[to])[1] * NG + g]
            if k:
                c_buf[mode, k] = value
                start(s3(mode, k))
            else:
                strip[mode, piece(g), :] = value

    def s3_done(mode):
        for k in range(1, NG):
            s3(mode, k).wait_recv()

    s2_to_s3(1)
    s2_to_s3(0)
    zg_finish()
    add_gram((z + 4) % NZ)

    def g1(mode, k):
        g, to = group(mode, k)
        dst = f[mode].at[t_of[mode] * NG + g_of[mode]]
        return remote(gram.at[mode, g], dst, g1_s, g1_r, mode * NG + k, to, z)

    for g in range(NG):
        gram[1, g] = lacc[:, g * TILE:(g + 1) * TILE].astype(BF16)
    for k in range(NG):
        for mode in range(2):
            g, _ = group(mode, k)
            if k:
                start(g1(mode, k))
            else:
                f[mode][t_of[mode] * NG + g] = gram[mode, g]

    def xr(j):
        return remote(strip.at[0, pl.ds(j * TILE, TILE), :], cross.at[j - 1], xr_s, xr_r, j, d, (z + j) % NZ)

    s3_done(0)
    for j in (1, 2, 3):
        start(xr(j))

    s3_done(1)
    zl_begin, zl_relay, zl_finish = ring(l_all, HALF, zl_s, zl_r, lambda span: strip.at[1, span, :])
    zl_begin()

    def g2(mode, direction, kind):
        k = 1 - 2 * direction
        _, to = other(mode, k + NT)
        half = direction if kind != 1 else 1 - direction
        t = t_of[mode] if kind < 2 else (t_of[mode] + NT - k) % NT
        span = f[mode].at[pl.ds(t * NG + half * (NG // 2), NG // 2)]
        return remote(span, span, g2_s, g2_r, (mode * 2 + direction) * 3 + kind, to, z)

    def g2_begin(mode):
        for k in range(1, NG):
            g1(mode, k).wait_recv()
        for kind in range(2):
            for direction in range(2):
                start(g2(mode, direction, kind))

    def g2_relay(mode):
        for direction in range(2):
            g2(mode, direction, 0).wait_recv()
            start(g2(mode, direction, 2))

    def g2_finish(mode):
        for direction in range(2):
            for kind in (1, 2):
                g2(mode, direction, kind).wait_recv()

    g2_begin(1)
    g2_begin(0)

    acc[...] = dot(gbuf[z], strip[0, 0:TILE, :])
    for j in range(1, 5):
        acc[...] += dot(gbuf[(z + j) % NZ], strip[0, j * TILE:(j + 1) * TILE, :])
    for j in (1, 2, 3):
        xr(j).wait_recv()
        acc[...] += dot(gbuf[(z + NZ - j) % NZ], cross[j - 1], 1, 1)
    for j in range(11):
        mext[j] = acc[(j % NZ) * TILE:(j % NZ + 1) * TILE, :].astype(BF16)

    pre[...] = jnp.zeros((NZ, TILE, TILE), F32)

    def add_shard(shard, s):
        direct = dot(shard, mext[s])
        for j in range(5):
            row = (s + j) % NZ
            pre[row] += direct[j * TILE:(j + 1) * TILE, :]
        three = mext[pl.ds(s + 1, 3)].reshape(3 * TILE, TILE)
        pre[s] += dot(shard[TILE:4 * TILE, :], three, 0, 0)

    zl_relay(1)
    g2_relay(1)
    g2_relay(0)
    add_shard(strip[1], z)
    zl_relay(2)
    add_shard(l_all[left], left)
    add_shard(l_all[right], right)

    def g3(mode, k):
        g, to = group(mode, k)
        dst = (gram_r, gram_l)[mode].at[g_of[mode]]
        return remote(h.at[mode, k], dst, g3_s, g3_r, mode * NG + k, to, z)

    def g2_to_g3(mode):
        g2_finish(mode)
        out = (gram_r, gram_l)[mode]
        for k in range(NG):
            g, to = group(mode, k)
            for q in range(NS):
                value = f[mode][source[mode, g * NS + q]]
                if k:
                    h[mode, k, q] = value
                else:
                    out[g, q] = value
            if k:
                start(g3(mode, k))

    zl_relay(3)
    g2_to_g3(1)
    g2_to_g3(0)
    add_shard(l_all[(z + 6) % NZ], (z + 6) % NZ)
    add_shard(l_all[(z + 2) % NZ], (z + 2) % NZ)
    add_shard(l_all[(z + 5) % NZ], (z + 5) % NZ)
    add_shard(l_all[(z + 3) % NZ], (z + 3) % NZ)
    zl_finish()
    add_shard(l_all[(z + 4) % NZ], (z + 4) % NZ)

    squares = jnp.zeros((8, TILE), F32)
    for a in range(NZ):
        rows = pre[a]
        squares = squares + jnp.sum((rows * rows).reshape(TILE // 8, 8, TILE), axis=0)
    norm_copies = share(1, squares)
    for copy in adam_copies + norm_copies:
        copy.wait_recv()

    def total(which):
        rows = jnp.sum(ps[which], axis=0)
        return jnp.sum(jnp.sum(rows, axis=0, keepdims=True), axis=1, keepdims=True)

    adam_sq = total(0).astype(BF16).astype(F32)
    scale = jnp.sqrt(adam_sq / (total(1) + norm_eps))
    for a in range(NZ):
        graft[a * TILE:(a + 1) * TILE, :] = (pre[a] * scale).astype(BF16)

    for mode in (1, 0):
        for k in range(1, NG):
            g3(mode, k).wait_recv()
    for copy in sent:
        copy.wait_send()


def update(owners, graft, momentum, gram_l, gram_r, left_stats, right_stats, step, momentum_out, left_out, right_out):
    new = beta_one * momentum[0] + (1.0 - beta_one) * graft[...].astype(F32)
    momentum_out[0] = new
    step[0] = (-step_rate * new).astype(BF16)
    own = lax.axis_index("dp")
    count = jnp.int32(0)
    for b in range(NBLK):
        count += jnp.where(owners[b] == own, 1, 0)
    for q in range(NS):
        on = count > q
        for stats, gram, out in ((left_stats, gram_l, left_out), (right_stats, gram_r, right_out)):
            for c in range(NG):
                cols = slice(c * TILE, (c + 1) * TILE)
                term = jnp.where(on, gram[c, q].astype(F32), 0.0)
                out[0, q, :, cols] = beta_stat * stats[0, q, :, cols] + (1.0 - beta_stat) * term


def body(grads, momentum, second_moment, owners, left_stats, right_stats, left_roots, right_roots):
    vmem = lambda shape, dtype=BF16: pltpu.VMEM(shape, dtype)
    dma = lambda n: pltpu.SemaphoreType.DMA((n,))
    hbm = pl.BlockSpec(memory_space=pltpu.MemorySpace.HBM)
    tile = (TILE, TILE)
    graft, gram_l, gram_r = pl.pallas_call(
        kernel,
        name="shampoo",
        out_shape=(
            jax.ShapeDtypeStruct((BS, TILE), BF16),
            jax.ShapeDtypeStruct((NG, NS) + tile, BF16),
            jax.ShapeDtypeStruct((NG, NS) + tile, BF16),
        ),
        in_specs=[pl.BlockSpec(memory_space=pltpu.SMEM)] + [hbm] * 4,
        out_specs=[pl.BlockSpec(memory_space=pltpu.VMEM)] * 3,
        scratch_shapes=[
            vmem((NZ, BS, TILE)), vmem((BS, TILE), F32), vmem((2, NS, HALF, TILE)),
            vmem((NG * NS, PIECE, TILE)), vmem((NG * NS, PIECE, TILE)), vmem((2, 3 * NG, PIECE, TILE)),
            vmem((NT * NG, PIECE, TILE)), vmem((NT * NG, PIECE, TILE)),
            vmem((2, NG, PIECE, TILE)), vmem((2, HALF, TILE)), vmem((3,) + tile),
            vmem((NZ, HALF, TILE)), vmem((2, NG) + tile), vmem((NT * NG,) + tile), vmem((NT * NG,) + tile), vmem((2, NG, NS) + tile),
            vmem((TILE, BS), F32), vmem((BS, TILE), F32), vmem((11,) + tile), vmem((TILE, BS)),
            vmem((NZ,) + tile, F32), vmem((2, NZ, 8, TILE), F32),
            pltpu.SMEM((NBLK,), jnp.int32), pltpu.SMEM((2, NG * NS), jnp.int32),
            dma(14), dma(4), dma(4), dma(8 * CH), dma(8 * CH), dma(8 * CH), dma(8 * CH), dma(2 * NZ), dma(2 * NZ),
            dma(2 * NG), dma(2 * NG), dma(2 * NT), dma(2 * NT), dma(2 * NG), dma(2 * NG),
            dma(2 * NG), dma(2 * NG), dma(12), dma(12), dma(2 * NG), dma(2 * NG),
        ],
        compiler_params=pltpu.CompilerParams(collective_id=0, has_side_effects=True, vmem_limit_bytes=60 * 2**20),
    )(owners, grads, second_moment, left_roots, right_roots)

    steps = 2
    rows, wide = TILE // steps, BS // steps
    slab = pl.BlockSpec((1, wide, TILE), lambda i: (0, i, 0))
    stats = pl.BlockSpec((1, NS, rows, BS), lambda i: (0, 0, i, 0))
    gram = pl.BlockSpec((NG, NS, rows, TILE), lambda i: (0, 0, i, 0))
    return pl.pallas_call(
        update,
        name="update",
        grid=(steps,),
        out_shape=(
            jax.ShapeDtypeStruct((1, BS, TILE), BF16),
            jax.ShapeDtypeStruct((1, BS, TILE), F32),
            jax.ShapeDtypeStruct((1, NS, TILE, BS), F32),
            jax.ShapeDtypeStruct((1, NS, TILE, BS), F32),
        ),
        in_specs=[
            pl.BlockSpec(memory_space=pltpu.SMEM),
            pl.BlockSpec((wide, TILE), lambda i: (i, 0)),
            slab, gram, gram, stats, stats,
        ],
        out_specs=(slab, slab, stats, stats),
        compiler_params=pltpu.CompilerParams(vmem_limit_bytes=60 * 2**20),
    )(owners, graft, momentum, gram_l, gram_r, left_stats, right_stats)


def solution(mesh):
    return jax.shard_map(
        body,
        mesh=mesh,
        in_specs=(
            P("dp", None, "mp"),
            P("dp", None, "mp"),
            P("dp", None, "mp"),
            P(),
            P("dp", None, "mp", None),
            P("dp", None, "mp", None),
            P("dp", None, None, "mp"),
            P("dp", None, None, "mp"),
        ),
        out_specs=(
            P("dp", None, "mp"),
            P("dp", None, "mp"),
            P("dp", None, "mp", None),
            P("dp", None, "mp", None),
        ),
        check_vma=False,
    )
```

time: 86.4 us -> 74.2 us (0.86)
  local copies, waits for them, and re-layouts: 5.85 us -> 0 us
  Pallas kernels: 76.9 us -> 73.5 us
  other arithmetic: 2.66 us -> 0 us
    unnamed x14 -> x0, local copies, waits for them, and re-layouts: 5.66 us -> none
    pallas_call x1, Pallas kernels: 73.7 us -> 69.3 us  [body(): pl.pallas_call(kernel, name='shampoo', out_shape=(jax.ShapeDtypeStruct((B...]
    reduce_sum x2 -> x0, other arithmetic: 1.12 us -> none  [the longest x1 0.97 us: routes(): jnp.sum((same & (ids[None, :] < ids[:, None])).astype(jnp.int32), axis=1)]
    pallas_call x1, Pallas kernels: 3.14 us -> 4.14 us  [body(): pl.pallas_call(update, name='update', grid=(steps,), out_shape=(jax.Shape...]
where the time goes in v2:
time: 74.2 us; the launch traced here: 74.1 us
  Pallas kernels  73.5 us (99%)
    pallas_call x1, Pallas kernels, body(): pl.pallas_call(kernel, name='shampoo', out_shape=(jax.ShapeDtypeStruct((B...  69.3 us
    pallas_call x1, Pallas kernels, body(): pl.pallas_call(update, name='update', grid=(steps,), out_shape=(jax.Shape...  4.14 us

profile of v2, /device:TPU:1, one launch (start us, length us, event | category | flops | bytes accessed | tf_op | source)
XLA Modules:
  0.0 74.1 jit_solution(16472190497709461942)
XLA Ops:
  0.6 69.3 %shampoo.1 = (bf16[1024,128]{1,0:T(8,128)(2,1)}, bf16[8,3,128,128]{3,2,1,0:T(8,128)(2,1)}, bf16[8,3,128,128]{3,2,1,0:T(8,128)(2,1)}) custom-call(s32[32]{0:T(128)} %owners.3, bf16[1,1024,128]{2,1,0:T(8,128)(2,1)} %grads.1, f32[1,1024,128]{2,1,0:T(8,128)} %second.1, bf16[1,3,1024,128]{3,2,1,0:T(8,128)(2,1)} %left_roots.1, bf16[1,3,1024,128]{3,2,1,0:T(8,128)(2,1)} %right_roots.1), custom_call_target="tpu_custom_call" | custom-call | tf_op jit(solution)/shard_map/shampoo/pallas_call | solution.py:440
  70.0 4.1 %update.1 = (bf16[1,1024,128]{2,1,0:T(8,128)(2,1)}, f32[1,1024,128]{2,1,0:T(8,128)}, f32[1,3,128,1024]{3,2,1,0:T(8,128)}, f32[1,3,128,1024]{3,2,1,0:T(8,128)}) custom-call(s32[32]{0:T(128)} %owners.3, bf16[1024,128]{1,0:T(8,128)(2,1)} %get-tuple-element.7.graft, f32[1,1024,128]{2,1,0:T(8,128)} %momentum.1, bf16[8,3,128,128]{3,2,1,0:T(8,128)(2,1)} %get-tuple-element.8.gram_l, ...), custom_call_target="tpu_custom_call" | custom-call | tf_op jit(solution)/shard_map/update/pallas_call | solution.py:471

commit v3 on v2

--- a/solution.py
+++ b/solution.py
@@ -40,8 +40,8 @@
 def kernel(
     owners, grads, second, left_roots, right_roots,
     graft, gram_l, gram_r,
-    gbuf, sec, rot, a_r, a_l, t_buf, b_r, b_l, c_buf, strip, cross,
-    l_all, gram, f_r, f_l, h, lacc, acc, mext, gt, pre, ps,
+    gbuf, sec, rot, a_r, a_l, t_buf, b_r, b_l, via, c_buf, strip, cross,
+    l_all, gram, f_r, f_l, h, lacc, acc, mext, gt, pre, ps, grafted,
     slot_of, source, local_sem, xr_s, xr_r, zg_s, zg_r, zl_s, zl_r, ps_s, ps_r, s1_s, s1_r, s2_s, s2_r, s3_s, s3_r, g1_s, g1_r, g2_s, g2_r, g3_s, g3_r,
 ):
     a, b, f = (a_r, a_l), (b_r, b_l), (f_r, f_l)
@@ -80,15 +80,18 @@
         return copy
 
     barrier = pltpu.get_barrier_semaphore()
-    partners = [(d, (z + k) % NZ) for k in range(1, NZ)]
+    partners = [(d, (z + k) % NZ) for k in (1, 7)]
     partners += [(group(0, k)[1], z) for k in range(1, NG)]
     for k in range(1, NT):
         for cc in range(2):
             partners.append((((y + k) % 4) * 8 + x * 2 + cc, z))
     for p in partners:
         pl.semaphore_signal(barrier, inc=1, device_id=p, device_id_type=MESH)
-    own_g = pltpu.make_async_copy(grads.at[0], gbuf.at[z], local_sem.at[0])
-    own_g.start()
+    def flush():
+        for copy in sent:
+            copy.wait_send()
+        sent.clear()
+
     strips = []
     for mode in (1, 0):
         for j in range(5):
@@ -100,6 +103,8 @@
             )
             copy.start()
             strips.append(copy)
+    own_g = pltpu.make_async_copy(grads.at[0], gbuf.at[z], local_sem.at[0])
+    own_g.start()
     own_sec = pltpu.make_async_copy(second.at[0], sec, local_sem.at[1])
     own_sec.start()
 
@@ -196,15 +201,7 @@
 
     adam_part = lax.fori_loop(0, BS // TILE, adam_rows, jnp.zeros((8, TILE), F32))
 
-    def share(which, part):
-        ps[which, z] = part
-        copies = []
-        for k in range(1, NZ):
-            i = which * NZ + k
-            copies.append(start(remote(ps.at[which, z], ps.at[which, z], ps_s, ps_r, i, d, (z + k) % NZ)))
-        return copies
-
-    adam_copies = share(0, adam_part)
+    ps[z, 0] = adam_part
     lax.fori_loop(0, NBLK, find_slot, 0)
     gt[...] = gbuf[z].T
     own_rows = pl.ds(pl.multiple_of(z * TILE, TILE), TILE)
@@ -217,30 +214,50 @@
     add_gram(z, True)
     zg_relay(1)
 
-    def s2(mode, k):
-        t, to = other(mode, k)
-        dst = b[mode].at[pl.ds(t_of[mode] * NG, NG)]
-        return remote(t_buf.at[mode, pl.ds((k - 1) * NG, NG)], dst, s2_s, s2_r, mode * NT + k, to, z)
+    def s2(mode, direction, kind):
+        _, to = other(mode, 1 - 2 * direction + NT)
+        half = (direction, 1 - direction, direction)[kind] * (NG // 2)
+        src = (16, 8 * direction, 8 * direction)[kind] + half
+        if kind == 0:
+            dst = via.at[mode, direction]
+        else:
+            dst = b[mode].at[pl.ds(8 + 8 * direction + half, NG // 2)]
+        i = (mode * 2 + direction) * 3 + kind
+        return remote(t_buf.at[mode, pl.ds(src, NG // 2)], dst, s2_s, s2_r, i, to, z)
+
+    def candidate(mode, g, t):
+        b_id = dev(mode, g, t)
+        g_owner, t_owner = place(mode, owners[b_id])
+        return a[mode][g_owner * NS + slot_of[b_id]], t_owner
 
     def s1_to_s2(mode):
         own_pieces[mode].wait()
         for k in range(1, NG):
             s1(mode, k).wait_recv()
-        for k in (1, 3, 2, 0):
-            t, _ = other(mode, k)
-
-            def choose(g, _):
-                b_id = dev(mode, g, t)
-                value = a[mode][place(mode, owners[b_id])[0] * NS + slot_of[b_id]]
-                if k == 0:
-                    b[mode][t * NG + g] = value
-                else:
-                    t_buf[mode, (k - 1) * NG + g] = value
-                return 0
-
-            lax.fori_loop(0, NG, choose, 0)
-            if k:
-                start(s2(mode, k))
+        opposite, _ = other(mode, 2)
+        for direction in range(2):
+            for g in range(4 * direction, 4 * direction + 4):
+                t_buf[mode, 16 + g] = candidate(mode, g, opposite)[0]
+            start(s2(mode, direction, 0))
+        for direction in range(2):
+            t, _ = other(mode, 1 - 2 * direction + NT)
+            for g in range(4 - 4 * direction, 8 - 4 * direction):
+                t_buf[mode, 8 * direction + g] = candidate(mode, g, t)[0]
+            start(s2(mode, direction, 1))
+        for g in range(NG):
+            b[mode][g] = candidate(mode, g, t_of[mode])[0]
+
+    def s2_merge(mode):
+        for direction in range(2):
+            s2(mode, direction, 0).wait_recv()
+            k = 1 - 2 * direction
+            t, _ = other(mode, k + NT)
+            behind, _ = other(mode, NT - k)
+            for i in range(4):
+                g = 4 * direction + i
+                value, t_owner = candidate(mode, g, t)
+                t_buf[mode, 8 * direction + g] = jnp.where(t_owner == behind, via[mode, direction, i], value)
+            start(s2(mode, direction, 2))
 
     s1_to_s2(1)
     s1_to_s2(0)
@@ -248,8 +265,11 @@
     add_gram(left)
     add_gram(right)
     zg_relay(2)
+    s2_merge(1)
+    s2_merge(0)
     add_gram((z + 6) % NZ)
     add_gram((z + 2) % NZ)
+    flush()
     zg_relay(3)
     add_gram((z + 5) % NZ)
     add_gram((z + 3) % NZ)
@@ -261,11 +281,14 @@
         )
 
     def s2_to_s3(mode):
-        for k in range(1, NT):
-            s2(mode, k).wait_recv()
+        for direction in range(2):
+            for kind in (1, 2):
+                s2(mode, direction, kind).wait_recv()
         for k in range(NG):
             g, to = group(mode, k)
-            value = b[mode][place(mode, owners[to])[1] * NG + g]
+            steps = (place(mode, owners[to])[1] + NT - t_of[mode]) % NT
+            side = jnp.where(steps == 3, 1, jnp.where(steps == 1, 2, jnp.where(g < 4, 1, 2)))
+            value = b[mode][jnp.where(steps == 0, 0, side) * NG + g]
             if k:
                 c_buf[mode, k] = value
                 start(s3(mode, k))
@@ -332,6 +355,7 @@
             for kind in (1, 2):
                 g2(mode, direction, kind).wait_recv()
 
+    flush()
     g2_begin(1)
     g2_begin(0)
 
@@ -367,6 +391,8 @@
         dst = (gram_r, gram_l)[mode].at[g_of[mode]]
         return remote(h.at[mode, k], dst, g3_s, g3_r, mode * NG + k, to, z)
 
+    own_out = []
+
     def g2_to_g3(mode):
         g2_finish(mode)
         out = (gram_r, gram_l)[mode]
@@ -374,16 +400,16 @@
             g, to = group(mode, k)
             for q in range(NS):
                 value = f[mode][source[mode, g * NS + q]]
-                if k:
-                    h[mode, k, q] = value
-                else:
-                    out[g, q] = value
+                h[mode, k, q] = value
             if k:
                 start(g3(mode, k))
-
-    zl_relay(3)
+            else:
+                own_out.append(pltpu.make_async_copy(h.at[mode, 0], out.at[g], local_sem.at[14 + mode]))
+                own_out[-1].start()
+
     g2_to_g3(1)
     g2_to_g3(0)
+    zl_relay(3)
     add_shard(l_all[(z + 6) % NZ], (z + 6) % NZ)
     add_shard(l_all[(z + 2) % NZ], (z + 2) % NZ)
     add_shard(l_all[(z + 5) % NZ], (z + 5) % NZ)
@@ -395,24 +421,28 @@
     for a in range(NZ):
         rows = pre[a]
         squares = squares + jnp.sum((rows * rows).reshape(TILE // 8, 8, TILE), axis=0)
-    norm_copies = share(1, squares)
-    for copy in adam_copies + norm_copies:
+    ps[z, 1] = squares
+    shares = [start(remote(ps.at[z], ps.at[z], ps_s, ps_r, k, d, (z + k) % NZ)) for k in (4, 3, 5, 2, 6, 1, 7)]
+    for copy in shares:
         copy.wait_recv()
 
     def total(which):
-        rows = jnp.sum(ps[which], axis=0)
+        rows = jnp.sum(ps[:, which], axis=0)
         return jnp.sum(jnp.sum(rows, axis=0, keepdims=True), axis=1, keepdims=True)
 
     adam_sq = total(0).astype(BF16).astype(F32)
     scale = jnp.sqrt(adam_sq / (total(1) + norm_eps))
     for a in range(NZ):
-        graft[a * TILE:(a + 1) * TILE, :] = (pre[a] * scale).astype(BF16)
+        grafted[a * TILE:(a + 1) * TILE, :] = (pre[a] * scale).astype(BF16)
+    own_out.append(pltpu.make_async_copy(grafted, graft, local_sem.at[16]))
+    own_out[-1].start()
 
     for mode in (1, 0):
         for k in range(1, NG):
             g3(mode, k).wait_recv()
-    for copy in sent:
-        copy.wait_send()
+    for copy in own_out:
+        copy.wait()
+    flush()
 
 
 def update(owners, graft, momentum, gram_l, gram_r, left_stats, right_stats, step, momentum_out, left_out, right_out):
@@ -446,18 +476,18 @@
             jax.ShapeDtypeStruct((NG, NS) + tile, BF16),
         ),
         in_specs=[pl.BlockSpec(memory_space=pltpu.SMEM)] + [hbm] * 4,
-        out_specs=[pl.BlockSpec(memory_space=pltpu.VMEM)] * 3,
+        out_specs=[hbm] * 3,
         scratch_shapes=[
             vmem((NZ, BS, TILE)), vmem((BS, TILE), F32), vmem((2, NS, HALF, TILE)),
             vmem((NG * NS, PIECE, TILE)), vmem((NG * NS, PIECE, TILE)), vmem((2, 3 * NG, PIECE, TILE)),
-            vmem((NT * NG, PIECE, TILE)), vmem((NT * NG, PIECE, TILE)),
+            vmem((3 * NG, PIECE, TILE)), vmem((3 * NG, PIECE, TILE)), vmem((2, 2, NG // 2, PIECE, TILE)),
             vmem((2, NG, PIECE, TILE)), vmem((2, HALF, TILE)), vmem((3,) + tile),
             vmem((NZ, HALF, TILE)), vmem((2, NG) + tile), vmem((NT * NG,) + tile), vmem((NT * NG,) + tile), vmem((2, NG, NS) + tile),
             vmem((TILE, BS), F32), vmem((BS, TILE), F32), vmem((11,) + tile), vmem((TILE, BS)),
-            vmem((NZ,) + tile, F32), vmem((2, NZ, 8, TILE), F32),
+            vmem((NZ,) + tile, F32), vmem((NZ, 2, 8, TILE), F32), vmem((BS, TILE)),
             pltpu.SMEM((NBLK,), jnp.int32), pltpu.SMEM((2, NG * NS), jnp.int32),
-            dma(14), dma(4), dma(4), dma(8 * CH), dma(8 * CH), dma(8 * CH), dma(8 * CH), dma(2 * NZ), dma(2 * NZ),
-            dma(2 * NG), dma(2 * NG), dma(2 * NT), dma(2 * NT), dma(2 * NG), dma(2 * NG),
+            dma(17), dma(4), dma(4), dma(8 * CH), dma(8 * CH), dma(8 * CH), dma(8 * CH), dma(NZ), dma(NZ),
+            dma(2 * NG), dma(2 * NG), dma(12), dma(12), dma(2 * NG), dma(2 * NG),
             dma(2 * NG), dma(2 * NG), dma(12), dma(12), dma(2 * NG), dma(2 * NG),
         ],
         compiler_params=pltpu.CompilerParams(collective_id=0, has_side_effects=True, vmem_limit_bytes=60 * 2**20),

time: 74.2 us -> 73.1 us (0.985)
  Pallas kernels: 73.5 us -> 72.4 us
    pallas_call x1, Pallas kernels: 69.3 us -> 68.2 us  [body(): pl.pallas_call(kernel, name='shampoo', out_shape=(jax.ShapeDtypeStruct((B...]
where the time goes in v3:
time: 73.1 us; the launch traced here: 73 us
  Pallas kernels  72.4 us (99%)
    pallas_call x1, Pallas kernels, body(): pl.pallas_call(kernel, name='shampoo', out_shape=(jax.ShapeDtypeStruct((B...  68.2 us
    pallas_call x1, Pallas kernels, body(): pl.pallas_call(update, name='update', grid=(steps,), out_shape=(jax.Shape...  4.14 us

profile of v3, /device:TPU:1, one launch (start us, length us, event | category | flops | bytes accessed | tf_op | source)
XLA Modules:
  0.0 73.0 jit_solution(17292298844846233714)
XLA Ops:
  0.6 68.2 %shampoo.1 = (bf16[1024,128]{1,0:T(8,128)(2,1)}, bf16[8,3,128,128]{3,2,1,0:T(8,128)(2,1)}, bf16[8,3,128,128]{3,2,1,0:T(8,128)(2,1)}) custom-call(s32[32]{0:T(128)} %owners.3, bf16[1,1024,128]{2,1,0:T(8,128)(2,1)} %grads.1, f32[1,1024,128]{2,1,0:T(8,128)} %second.1, bf16[1,3,1024,128]{3,2,1,0:T(8,128)(2,1)} %left_roots.1, bf16[1,3,1024,128]{3,2,1,0:T(8,128)(2,1)} %right_roots.1), custom_call_target="tpu_custom_call" | custom-call | tf_op jit(solution)/shard_map/shampoo/pallas_call | solution.py:470
  68.9 4.1 %update.1 = (bf16[1,1024,128]{2,1,0:T(8,128)(2,1)}, f32[1,1024,128]{2,1,0:T(8,128)}, f32[1,3,128,1024]{3,2,1,0:T(8,128)}, f32[1,3,128,1024]{3,2,1,0:T(8,128)}) custom-call(s32[32]{0:T(128)} %owners.3, bf16[1024,128]{1,0:T(8,128)(2,1)} %get-tuple-element.7.graft, f32[1,1024,128]{2,1,0:T(8,128)} %momentum.1, bf16[8,3,128,128]{3,2,1,0:T(8,128)(2,1)} %get-tuple-element.8.gram_l, ...), custom_call_target="tpu_custom_call" | custom-call | tf_op jit(solution)/shard_map/update/pallas_call | solution.py:501

commit v4 on v3

--- a/solution.py
+++ b/solution.py
@@ -22,6 +22,7 @@
 BS = 1024
 HALF = 5 * TILE
 PIECE = HALF // NG
+FAR = (4, 3, 5, 2, 6, 1, 7)
 CH = 2
 F32 = jnp.float32
 BF16 = jnp.bfloat16
@@ -185,7 +186,7 @@
             )
         )
         own_pieces[mode].start()
-    for k in range(1, NG):
+    for k in FAR:
         start(s1(1, k))
         start(s1(0, k))
 
@@ -269,7 +270,6 @@
     s2_merge(0)
     add_gram((z + 6) % NZ)
     add_gram((z + 2) % NZ)
-    flush()
     zg_relay(3)
     add_gram((z + 5) % NZ)
     add_gram((z + 3) % NZ)
@@ -284,7 +284,7 @@
         for direction in range(2):
             for kind in (1, 2):
                 s2(mode, direction, kind).wait_recv()
-        for k in range(NG):
+        for k in FAR + (0,):
             g, to = group(mode, k)
             steps = (place(mode, owners[to])[1] + NT - t_of[mode]) % NT
             side = jnp.where(steps == 3, 1, jnp.where(steps == 1, 2, jnp.where(g < 4, 1, 2)))
@@ -311,7 +311,7 @@
 
     for g in range(NG):
         gram[1, g] = lacc[:, g * TILE:(g + 1) * TILE].astype(BF16)
-    for k in range(NG):
+    for k in FAR + (0,):
         for mode in range(2):
             g, _ = group(mode, k)
             if k:
@@ -355,7 +355,6 @@
             for kind in (1, 2):
                 g2(mode, direction, kind).wait_recv()
 
-    flush()
     g2_begin(1)
     g2_begin(0)
 
@@ -396,7 +395,7 @@
     def g2_to_g3(mode):
         g2_finish(mode)
         out = (gram_r, gram_l)[mode]
-        for k in range(NG):
+        for k in FAR + (0,):
             g, to = group(mode, k)
             for q in range(NS):
                 value = f[mode][source[mode, g * NS + q]]

time: 73.1 us -> 70 us (0.958)
  the two profiles are of different devices: /device:TPU:1 before, /device:TPU:32 now
where the time goes in v4:
time: 70 us; the launch traced here: 69.9 us
  Pallas kernels  69.2 us (99%)
    pallas_call x1, Pallas kernels, body(): pl.pallas_call(kernel, name='shampoo', out_shape=(jax.ShapeDtypeStruct((B...  65.1 us
    pallas_call x1, Pallas kernels, body(): pl.pallas_call(update, name='update', grid=(steps,), out_shape=(jax.Shape...  4.14 us

profile of v4, /device:TPU:32, one launch (start us, length us, event | category | flops | bytes accessed | tf_op | source)
XLA Modules:
  0.0 69.9 jit_solution(10292801044496450474)
XLA Ops:
  0.6 65.1 %shampoo.1 = (bf16[1024,128]{1,0:T(8,128)(2,1)}, bf16[8,3,128,128]{3,2,1,0:T(8,128)(2,1)}, bf16[8,3,128,128]{3,2,1,0:T(8,128)(2,1)}) custom-call(s32[32]{0:T(128)} %owners.3, bf16[1,1024,128]{2,1,0:T(8,128)(2,1)} %grads.1, f32[1,1024,128]{2,1,0:T(8,128)} %second.1, bf16[1,3,1024,128]{3,2,1,0:T(8,128)(2,1)} %left_roots.1, bf16[1,3,1024,128]{3,2,1,0:T(8,128)(2,1)} %right_roots.1), custom_call_target="tpu_custom_call" | custom-call | tf_op jit(solution)/shard_map/shampoo/pallas_call | solution.py:469
  65.7 4.1 %update.1 = (bf16[1,1024,128]{2,1,0:T(8,128)(2,1)}, f32[1,1024,128]{2,1,0:T(8,128)}, f32[1,3,128,1024]{3,2,1,0:T(8,128)}, f32[1,3,128,1024]{3,2,1,0:T(8,128)}) custom-call(s32[32]{0:T(128)} %owners.3, bf16[1024,128]{1,0:T(8,128)(2,1)} %get-tuple-element.7.graft, f32[1,1024,128]{2,1,0:T(8,128)} %momentum.1, bf16[8,3,128,128]{3,2,1,0:T(8,128)(2,1)} %get-tuple-element.8.gram_l, ...), custom_call_target="tpu_custom_call" | custom-call | tf_op jit(solution)/shard_map/update/pallas_call | solution.py:500

commit v5 on v4

--- a/solution.py
+++ b/solution.py
@@ -262,7 +262,6 @@
 
     s1_to_s2(1)
     s1_to_s2(0)
-    lax.fori_loop(0, NG, find_blocks, 0)
     add_gram(left)
     add_gram(right)
     zg_relay(2)
@@ -271,6 +270,7 @@
     add_gram((z + 6) % NZ)
     add_gram((z + 2) % NZ)
     zg_relay(3)
+    lax.fori_loop(0, NG, find_blocks, 0)
     add_gram((z + 5) % NZ)
     add_gram((z + 3) % NZ)
 

time: 70 us -> 68.6 us (0.980)
  Pallas kernels: 69.2 us -> 67.8 us
    pallas_call x1, Pallas kernels: 65.1 us -> 63.7 us  [body(): pl.pallas_call(kernel, name='shampoo', out_shape=(jax.ShapeDtypeStruct((B...]
where the time goes in v5:
time: 68.6 us; the launch traced here: 68.4 us
  Pallas kernels  67.8 us (99%)
    pallas_call x1, Pallas kernels, body(): pl.pallas_call(kernel, name='shampoo', out_shape=(jax.ShapeDtypeStruct((B...  63.7 us
    pallas_call x1, Pallas kernels, body(): pl.pallas_call(update, name='update', grid=(steps,), out_shape=(jax.Shape...  4.14 us

profile of v5, /device:TPU:32, one launch (start us, length us, event | category | flops | bytes accessed | tf_op | source)
XLA Modules:
  0.0 68.4 jit_solution(17587380907592650362)
XLA Ops:
  0.6 63.7 %shampoo.1 = (bf16[1024,128]{1,0:T(8,128)(2,1)}, bf16[8,3,128,128]{3,2,1,0:T(8,128)(2,1)}, bf16[8,3,128,128]{3,2,1,0:T(8,128)(2,1)}) custom-call(s32[32]{0:T(128)} %owners.3, bf16[1,1024,128]{2,1,0:T(8,128)(2,1)} %grads.1, f32[1,1024,128]{2,1,0:T(8,128)} %second.1, bf16[1,3,1024,128]{3,2,1,0:T(8,128)(2,1)} %left_roots.1, bf16[1,3,1024,128]{3,2,1,0:T(8,128)(2,1)} %right_roots.1), custom_call_target="tpu_custom_call" | custom-call | tf_op jit(solution)/shard_map/shampoo/pallas_call | solution.py:469
  64.3 4.1 %update.1 = (bf16[1,1024,128]{2,1,0:T(8,128)(2,1)}, f32[1,1024,128]{2,1,0:T(8,128)}, f32[1,3,128,1024]{3,2,1,0:T(8,128)}, f32[1,3,128,1024]{3,2,1,0:T(8,128)}) custom-call(s32[32]{0:T(128)} %owners.3, bf16[1024,128]{1,0:T(8,128)(2,1)} %get-tuple-element.7.graft, f32[1,1024,128]{2,1,0:T(8,128)} %momentum.1, bf16[8,3,128,128]{3,2,1,0:T(8,128)(2,1)} %get-tuple-element.8.gram_l, ...), custom_call_target="tpu_custom_call" | custom-call | tf_op jit(solution)/shard_map/update/pallas_call | solution.py:500
